TPU v7x, 32 devices: a whole 2x2x4 slice. The times are simulated.
32 devices in a mesh: bed: 8 (over y, x, core), layer: 4 (over z).
Axes of the slice: x: 2, y: 2, z: 4, core: 2. Of those that a mesh axis runs over, the one named last changes fastest.
Arguments:
- concentration: float32 [8, 1024, 4096], P('layer', 'bed'), may hold values from 0.2 to 2
- east_velocity: bfloat16 [8, 1024, 4096], P('layer', 'bed'), may hold values from -3 to 3
- north_velocity: bfloat16 [8, 1024, 4096], P('layer', 'bed'), may hold values from -3 to 3
- settling: float32 [1024, 4096], P('bed'), may hold values from 0.02 to 0.15
- surface: float32 [1024, 4096], P('bed'), may hold values from 1.8 to 6
- bed_level: float32 [1024, 4096], P('bed'), may hold values from -1 to 1
- erosion: float32 [1024, 4096], P('bed'), may hold values from 0 to 0.08
- wet_mask: int32 [1024, 4096], P('bed'), may hold values 0 or 1
Outputs:
- new_concentration: float32 [8, 1024, 4096], P('layer', 'bed')
- new_bed: float32 [1024, 4096], P('bed')
Inputs may be any that keep to these rules, and one draw needn't show every extreme that they name: `wet_mask`: 1 marks a wet cell, 0 a dry one.
All inputs are finite; a program needn't handle non-finite values. No bound on the sum of `wet_mask` on one device may be relied on, other than what follows from the above.
Results may differ from a plain program's by a relative error of at most 0.0003.
Values sent between devices are 32-bit elements; how exact they have to be, the bound alone decides.
A program may use at most 128 MiB of HBM per device.

v0:
```python
import jax
import jax.numpy as jnp
from jax import lax
from jax.sharding import PartitionSpec as P

SWEEPS = 4


ADVECT_RATE = 0.1
FLUX_GAIN = 0.15
POROSITY_GAIN = 1.0 / 0.6
RELAX_RATE = 0.2
CRIT_SLOPE = 0.5
DEPTH_FLOOR = 1.0


def padded(block, sides, width):
    for axis, dim in sides:
        count = lax.axis_size(axis)
        forward = [(i, i + 1) for i in range(count - 1)]
        backward = [(target, source) for source, target in forward]
        low = lax.ppermute(
            lax.slice_in_dim(block, block.shape[dim] - width, None, axis=dim), axis, forward
        )
        high = lax.ppermute(lax.slice_in_dim(block, 0, width, axis=dim), axis, backward)
        block = jnp.concatenate([low, block, high], axis=dim)
    return block


def passed_along(block, axis, distance):
    devices = range(lax.axis_size(axis))
    route = [(i - distance, i) for i in devices if i - distance in devices]
    return lax.ppermute(block, axis, route)


def face_divergence(values, speeds, which_axis):
    length_here = values.shape[which_axis]
    left_val = lax.slice_in_dim(values, 0, length_here - 1, axis=which_axis)
    right_val = lax.slice_in_dim(values, 1, length_here, axis=which_axis)
    left_spd = lax.slice_in_dim(speeds, 0, length_here - 1, axis=which_axis)
    right_spd = lax.slice_in_dim(speeds, 1, length_here, axis=which_axis)
    face_speed = 0.5 * (left_spd + right_spd)
    face_flux = jnp.maximum(face_speed, 0.0) * left_val + jnp.minimum(face_speed, 0.0) * right_val
    return lax.slice_in_dim(face_flux, 1, length_here - 1, axis=which_axis) - lax.slice_in_dim(
        face_flux, 0, length_here - 2, axis=which_axis
    )


def slide_sweep(height, wetness):
    drop_x = height[:-1, :] - height[1:, :]
    move_x = (
        RELAX_RATE
        * (drop_x - jnp.clip(drop_x, -CRIT_SLOPE, CRIT_SLOPE))
        * wetness[:-1, :]
        * wetness[1:, :]
    )
    drop_y = height[:, :-1] - height[:, 1:]
    move_y = (
        RELAX_RATE
        * (drop_y - jnp.clip(drop_y, -CRIT_SLOPE, CRIT_SLOPE))
        * wetness[:, :-1]
        * wetness[:, 1:]
    )
    return (
        height[1:-1, 1:-1]
        - move_x[1:, 1:-1]
        + move_x[:-1, 1:-1]
        - move_y[1:-1, 1:]
        + move_y[1:-1, :-1]
    )


def edge_pair(field):
    return jnp.concatenate([field[:, :1], field[:, -1:]], 1)


def body(
    concentration, east_velocity, north_velocity, settling, surface, bed_level, erosion, wet_mask
):
    layers_here = concentration.shape[0]
    layer_count = layers_here * lax.axis_size("layer")
    layer_index = lax.axis_index("layer")
    water_depth = surface - bed_level
    layer_thick = water_depth / layer_count
    east_speed = east_velocity.astype(jnp.float32)
    north_speed = north_velocity.astype(jnp.float32)
    flux_east = east_speed * concentration * layer_thick
    flux_north = north_speed * concentration * layer_thick
    edges = jnp.stack([edge_pair(concentration), edge_pair(east_speed), edge_pair(flux_east)])
    rims = padded(edges, (("bed", 2),), 1)
    before = rims[:, :, :1]
    after = rims[:, :, 3:]
    conc_along = jnp.concatenate([before[0], concentration, after[0]], 1)
    speed_along = jnp.concatenate([before[1], east_speed, after[1]], 1)
    east_wide = jnp.concatenate([before[2], flux_east, after[2]], 1)
    upper_row = passed_along(concentration[0], "layer", -1)
    pad_y = ((0, 0), (0, 0), (1, 1))
    advect = face_divergence(conc_along, speed_along, 1) + face_divergence(
        jnp.pad(concentration, pad_y), jnp.pad(north_speed, pad_y), 2
    )
    bottom_flag = (layer_index == 0).astype(jnp.float32)
    falling = jnp.concatenate([concentration[1:], upper_row[None]], 0) * settling
    source = falling - settling * concentration
    source = source.at[0].add(bottom_flag * erosion)
    settled = concentration - ADVECT_RATE * advect + layer_count / water_depth * source
    north_wide = jnp.pad(flux_north, pad_y)
    spread = 0.5 * (
        east_wide[:, 2:, :] - east_wide[:, :-2, :] + north_wide[:, :, 2:] - north_wide[:, :, :-2]
    )
    bed_change = FLUX_GAIN * jnp.sum(spread, 0) - bottom_flag * settling * concentration[0]
    wet_float = wet_mask.astype(jnp.float32)
    rim_width, rounds = (1, SWEEPS)
    summed_flux = lax.psum(bed_change, "layer")
    height = bed_level - POROSITY_GAIN * wet_float * (summed_flux + erosion)
    side_pad = ((0, 0), (rim_width, rim_width))
    wet_wide = jnp.pad(padded(wet_float, (("bed", 0),), rim_width), side_pad)
    for round_index in range(rounds):
        height_wide = jnp.pad(padded(height, (("bed", 0),), rim_width), side_pad)
        wetness = wet_wide
        height_wide = slide_sweep(height_wide, wetness)
        wetness = wetness[1:-1, 1:-1]
        height = height_wide
    new_depth = jnp.maximum(surface - height, DEPTH_FLOOR)
    return (settled * (water_depth / new_depth), height)


def solution(mesh):
    in_specs = (
        P("layer", "bed", None),
        P("layer", "bed", None),
        P("layer", "bed", None),
        P("bed", None),
        P("bed", None),
        P("bed", None),
        P("bed", None),
        P("bed", None),
    )
    out_specs = (P("layer", "bed", None), P("bed", None))
    return jax.shard_map(body, mesh=mesh, in_specs=in_specs, out_specs=out_specs, check_vma=False)
```

profile of v0, /device:TPU:4, one launch (start us, length us, event | category | flops | bytes accessed | tf_op | source)
XLA Modules:
  0.0 256.3 jit_solution(9465956623220491633)
XLA Ops:
  7.2 2.7 %fusion.39 = (f32[1,128,4096]{2,1,0:T(8,128)S(1)}, f32[128,4096]{1,0:T(8,128)S(1)}) fusion(f32[2,128,4096]{2,1,0:T(8,128)} %param.10), kind=kLoop, calls=%fused_computation.111 | loop fusion | bytes 8388608 | tf_op jit(solution)/shard_map/slice | solution.py:102
  11.9 3.4 %broadcast_divide_fusion = (f32[128,4096]{1,0:T(8,128)}, f32[128,4096]{1,0:T(8,128)S(1)}) fusion(f32[128,4096]{1,0:T(8,128)} %param.14, f32[128,4096]{1,0:T(8,128)S(1)} %copy-done.16), kind=kLoop, calls=%fused_computation.99 | loop fusion | flops 1048576 | bytes 8388608 | tf_op jit(solution)/shard_map/div | solution.py:105
  16.8 42.6 %collective-permute-done.2 = f32[128,4096]{1,0:T(8,128)S(1)} collective-permute-done((f32[128,4096]{1,0:T(8,128)S(1)}, f32[128,4096]{1,0:T(8,128)S(1)}, u32[]{:S(2)}, u32[]{:S(2)}) %collective-permute-start.2) | collective-permute-done | bytes 2097184 | tf_op jit(solution)/shard_map/ppermute | solution.py:33
  59.5 4.4 %multiply_multiply_fusion = (f32[2,128,4096]{2,1,0:T(8,128)}, f32[2,128,4096]{2,1,0:T(8,128)S(1)}, f32[2,128,4096]{2,1,0:T(8,128)}) fusion(f32[2,128,4096]{2,1,0:T(8,128)S(1)} %copy-done, f32[128,4096]{1,0:T(8,128)S(1)} %broadcast_multiply_fusion, bf16[2,128,4096]{2,1,0:T(8,128)(2,1)S(1)} %copy-done.11, bf16[2,128,4096]{2,1,0:T(8,128)(2,1)S(1)} %copy-done.8, ...), kind=kLoop, calls=%fused_computation.22 | loop fusion | flops 10485760 | bytes 29360128 | tf_op jit(solution)/shard_map/mul | solution.py:88
  63.9 2.0 copy-done.6
  66.3 1.9 collective-permute-start.1
  68.2 2.4 collective-permute-start
  70.7 4.4 %collective-permute-done = f32[3,2,1,4096]{3,2,1,0:T(1,128)S(1)} collective-permute-done((f32[3,2,1,4096]{3,2,1,0:T(1,128)S(1)}, f32[3,2,1,4096]{3,2,1,0:T(1,128)S(1)}, u32[]{:S(2)}, u32[]{:S(2)}) %collective-permute-start) | collective-permute-done | bytes 98336 | tf_op jit(solution)/shard_map/ppermute | solution.py:22
  75.1 8.3 %fusion.6 = f32[128,4096]{1,0:T(8,128)S(1)} fusion(f32[2,128,4096]{2,1,0:T(8,128)} %copy-done.6, f32[2,1,4096]{2,1,0:T(1,128)S(1)} %get-tuple-element.44, f32[2,1,4096]{2,1,0:T(1,128)S(1)} %get-tuple-element.41, f32[2,128,4096]{2,1,0:T(8,128)} %get-tuple-element.18), kind=kLoop, calls=%fused_computation.11 | loop fusion | flops 6815744 | bytes 10551296 | tf_op jit(solution)/shard_map/reduce_sum | solution.py:110
  85.3 1.9 convert_element_type.25
  88.6 1.9 collective-permute-start.5
  90.6 4.5 %collective-permute-start.6 = (f32[1,4096]{1,0:T(1,128)S(1)}, f32[1,4096]{1,0:T(1,128)S(1)}, u32[]{:S(2)}, u32[]{:S(2)}) collective-permute-start(f32[1,4096]{1,0:T(1,128)S(1)} %get-tuple-element.34), channel_id=1, source_target_pairs={{4,0},{8,4},{12,8},{16,12},{20,16},{24,20},{28,24},{5,1},{9,5},{13... | collective-permute-start | bytes 49160 | tf_op jit(solution)/shard_map/ppermute | solution.py:25
  95.1 2.5 convert_element_type.23
  97.6 73.6 %all-reduce.10.cloned.1.call-done = f32[128,4096]{1,0:T(8,128)} async-done(((f32[128,4096]{1,0:T(8,128)}), f32[128,4096]{1,0:T(8,128)}) %all-reduce.10.cloned.1.call-update) | async-done | bytes 2097168 | tf_op jit(solution)/shard_map/psum | solution.py:113
  171.2 4.2 %multiply_subtract_fusion = f32[128,4096]{1,0:T(8,128)S(1)} fusion(f32[128,4096]{1,0:T(8,128)} %param.15, f32[128,4096]{1,0:T(8,128)} %all-reduce.10.cloned.1.call-done, f32[128,4096]{1,0:T(8,128)} %param.16, s32[128,4096]{1,0:T(8,128)} %param.17), kind=kLoop, calls=%fused_computation.96 | loop fusion | flops 2621440 | bytes 10485760 | tf_op jit(solution)/shard_map/sub | solution.py:114
  175.5 1.9 collective-permute-start.3
  177.4 4.5 %collective-permute-start.4 = (f32[1,4096]{1,0:T(1,128)S(1)}, f32[1,4096]{1,0:T(1,128)S(1)}, u32[]{:S(2)}, u32[]{:S(2)}) collective-permute-start(f32[1,4096]{1,0:T(1,128)S(1)} %get-tuple-element.36), channel_id=1, source_target_pairs={{4,0},{8,4},{12,8},{16,12},{20,16},{24,20},{28,24},{5,1},{9,5},{13... | collective-permute-start | bytes 49160 | tf_op jit(solution)/shard_map/ppermute | solution.py:25
  188.0 2.7 %collective-permute-start.7 = (f32[1,4096]{1,0:T(1,128)S(1)}, f32[1,4096]{1,0:T(1,128)S(1)}, u32[]{:S(2)}, u32[]{:S(2)}) collective-permute-start(f32[1,4096]{1,0:T(1,128)S(1)} %get-tuple-element.31), channel_id=1, source_target_pairs={{0,4},{4,8},{8,12},{12,16},{16,20},{20,24},{24,28},{1,5},{5,9},{9,... | collective-permute-start | bytes 49160 | tf_op jit(solution)/shard_map/ppermute | solution.py:22
  190.8 4.1 %collective-permute-start.8 = (f32[1,4096]{1,0:T(1,128)S(1)}, f32[1,4096]{1,0:T(1,128)S(1)}, u32[]{:S(2)}, u32[]{:S(2)}) collective-permute-start(f32[1,4096]{1,0:T(1,128)S(1)} %get-tuple-element.32), channel_id=1, source_target_pairs={{4,0},{8,4},{12,8},{16,12},{20,16},{24,20},{28,24},{5,1},{9,5},{13... | collective-permute-start | bytes 49160 | tf_op jit(solution)/shard_map/ppermute | solution.py:25
  194.9 2.4 multiply_add_fusion
  197.3 2.5 convert_element_type.22
  204.4 2.4 collective-permute-start.10
  206.8 1.9 collective-permute-start.9
  209.4 3.4 %collective-permute-done.9 = f32[1,4096]{1,0:T(1,128)S(1)} collective-permute-done((f32[1,4096]{1,0:T(1,128)S(1)}, f32[1,4096]{1,0:T(1,128)S(1)}, u32[]{:S(2)}, u32[]{:S(2)}) %collective-permute-start.9) | collective-permute-done | bytes 16416 | tf_op jit(solution)/shard_map/ppermute | solution.py:22
  215.6 1.9 slice_add_fusion.2
  217.5 1.9 collective-permute-start.11
  219.4 4.8 %collective-permute-start.12 = (f32[1,4096]{1,0:T(1,128)S(1)}, f32[1,4096]{1,0:T(1,128)S(1)}, u32[]{:S(2)}, u32[]{:S(2)}) collective-permute-start(f32[1,4096]{1,0:T(1,128)S(1)} %get-tuple-element.28), channel_id=1, source_target_pairs={{4,0},{8,4},{12,8},{16,12},{20,16},{24,20},{28,24},{5,1},{9,5},{13... | collective-permute-start | bytes 49160 | tf_op jit(solution)/shard_map/ppermute | solution.py:25
  224.2 5.1 %fusion.1 = f32[2,129,4096]{2,1,0:T(8,128)S(1)} fusion(f32[2,128,4096]{2,1,0:T(8,128)S(1)} %copy-done.2, f32[2,1,4096]{2,1,0:T(1,128)S(1)} %get-tuple-element.45, f32[2,1,4096]{2,1,0:T(1,128)S(1)} %get-tuple-element.42, f32[2,1,4096]{2,1,0:T(1,128)S(1)} %get-tuple-element.43, f32[2,128,4096]{2,1,0:T(8,128)} %convert_element_type.22, ...), kind=kLoop, calls=%fused_computation.3 | loop fusion | flops 11624448 | bytes 12746752 | tf_op jit(solution)/shard_map/add | solution.py:43
  230.0 2.2 fusion.33
  232.2 2.6 %fusion.36 = f32[130,4097]{1,0:T(8,128)} fusion(f32[130,4098]{1,0:T(8,128)S(1)} %select_maximum_fusion, f32[130,4098]{1,0:T(8,128)S(1)} %select_maximum_fusion.6), kind=kLoop, calls=%fused_computation.57 | loop fusion | flops 3195660 | bytes 10652200 | tf_op jit(solution)/shard_map/mul | solution.py:59
  234.9 9.2 %maximum_divide_fusion = (f32[128,4096]{1,0:T(8,128)}, f32[128,4096]{1,0:T(8,128)}) fusion(f32[128,4096]{1,0:T(8,128)} %copy-done.5, f32[128,4096]{1,0:T(8,128)} %param.14, f32[130,4097]{1,0:T(8,128)} %fusion.36, f32[129,4098]{1,0:T(8,128)} %fusion.33, f32[128,4096]{1,0:T(8,128)} %copy-done.4), kind=kLoop, calls=%fused_computation.95 | loop fusion | flops 3670016 | bytes 18874368 | tf_op jit(solution)/shard_map/div | solution.py:124
  244.0 5.4 %fusion.11 = f32[2,128,4096]{2,1,0:T(8,128)} fusion(f32[2,128,4096]{2,1,0:T(8,128)S(1)} %copy-done.2, f32[2,128,4097]{2,1,0:T(8,128)S(1)} %multiply_add_fusion, f32[2,129,4096]{2,1,0:T(8,128)S(1)} %fusion.1, f32[2,128,4096]{2,1,0:T(8,128)S(1)} %fusion.38, f32[128,4096]{1,0:T(8,128)} %get-tuple-element.16, f32[128,4096]{1,0:T(8,128)} %get-tuple-element.14), kind=kLoop, calls=%fused_computation.18 | loop fusion | flops 8388608 | bytes 33554432 | tf_op jit(solution)/shard_map/mul | solution.py:124
  (76 shorter events, 21.9 us)
Async XLA Ops:
  7.2 4.4 %copy-start.8 = (bf16[2,128,4096]{2,1,0:T(8,128)(2,1)S(1)}, bf16[2,128,4096]{2,1,0:T(8,128)(2,1)}, u32[]{:S(2)}) copy-start(bf16[2,128,4096]{2,1,0:T(8,128)(2,1)} %param.11) | copy-start | bytes 6291460
  7.2 164.1 %all-reduce.10.cloned.1.call-start = ((), (), s32[]{:S(2)}) async-start(), calls=%async_computation | async-start | bytes 4194304 | tf_op jit(solution)/shard_map/psum | solution.py:113
  7.2 4.3 %copy-start = (f32[2,128,4096]{2,1,0:T(8,128)S(1)}, f32[2,128,4096]{2,1,0:T(8,128)}, u32[]{:S(2)}) copy-start(f32[2,128,4096]{2,1,0:T(8,128)} %param.10) | copy-start | bytes 12582916
  7.2 4.7 %copy-start.16 = (f32[128,4096]{1,0:T(8,128)S(1)}, f32[128,4096]{1,0:T(8,128)}, u32[]{:S(2)}) copy-start(f32[128,4096]{1,0:T(8,128)} %param.15) | copy-start | bytes 6291460
  9.9 49.5 %collective-permute-start.2 = (f32[128,4096]{1,0:T(8,128)S(1)}, f32[128,4096]{1,0:T(8,128)S(1)}, u32[]{:S(2)}, u32[]{:S(2)}) collective-permute-start(f32[128,4096]{1,0:T(8,128)S(1)} %get-tuple-element.22), channel_id=1, source_target_pairs={{1,0},{2,1},{3,2},{5,4},{6,5},{7,6},{9,8},{10,9},{11,10},{13,12},{... | collective-permute-start | bytes 6291464 | tf_op jit(solution)/shard_map/ppermute | solution.py:33
  15.3 1.3 copy-start.5
  15.3 44.2 %copy-start.11 = (bf16[2,128,4096]{2,1,0:T(8,128)(2,1)S(1)}, bf16[2,128,4096]{2,1,0:T(8,128)(2,1)}, u32[]{:S(2)}) copy-start(bf16[2,128,4096]{2,1,0:T(8,128)(2,1)} %param.12) | copy-start | bytes 6291460
  15.3 44.2 %copy-start.13 = (f32[128,4096]{1,0:T(8,128)S(1)}, f32[128,4096]{1,0:T(8,128)}, u32[]{:S(2)}) copy-start(f32[128,4096]{1,0:T(8,128)} %param.13) | copy-start | bytes 6291460
  63.9 2.0 copy-start.6
  66.3 4.4 %collective-permute-start.1 = (f32[3,2,1,4096]{3,2,1,0:T(1,128)S(1)}, f32[3,2,1,4096]{3,2,1,0:T(1,128)S(1)}, u32[]{:S(2)}, u32[]{:S(2)}) collective-permute-start(f32[3,2,1,4096]{3,2,1,0:T(1,128)S(1)} %get-tuple-element.39), channel_id=1, source_target_pairs={{4,0},{8,4},{12,8},{16,12},{20,16},{24,20},{28,24},{5,1},{9,5},{13... | collective-permute-start | bytes 294920 | tf_op jit(solution)/shard_map/ppermute | solution.py:25
  68.2 6.8 %collective-permute-start = (f32[3,2,1,4096]{3,2,1,0:T(1,128)S(1)}, f32[3,2,1,4096]{3,2,1,0:T(1,128)S(1)}, u32[]{:S(2)}, u32[]{:S(2)}) collective-permute-start(f32[3,2,1,4096]{3,2,1,0:T(1,128)S(1)} %get-tuple-element.40), channel_id=1, source_target_pairs={{0,4},{4,8},{8,12},{12,16},{16,20},{20,24},{24,28},{1,5},{5,9},{9,... | collective-permute-start | bytes 294920 | tf_op jit(solution)/shard_map/ppermute | solution.py:22
  75.1 8.3 %copy-start.1 = (f32[2,128,4096]{2,1,0:T(8,128)S(1)}, f32[2,128,4096]{2,1,0:T(8,128)}, u32[]{:S(2)}) copy-start(f32[2,128,4096]{2,1,0:T(8,128)} %param.10) | copy-start | bytes 12582916
  75.1 8.3 %copy-start.14 = (f32[128,4096]{1,0:T(8,128)S(1)}, f32[128,4096]{1,0:T(8,128)}, u32[]{:S(2)}) copy-start(f32[128,4096]{1,0:T(8,128)} %param.13) | copy-start | bytes 6291460
  85.3 9.8 %copy-start.12 = (bf16[2,128,4096]{2,1,0:T(8,128)(2,1)S(1)}, bf16[2,128,4096]{2,1,0:T(8,128)(2,1)}, u32[]{:S(2)}) copy-start(bf16[2,128,4096]{2,1,0:T(8,128)(2,1)} %param.12) | copy-start | bytes 6291460
  87.2 1.4 copy-start.9
  88.6 93.3 %collective-permute-start.5 = (f32[1,4096]{1,0:T(1,128)S(1)}, f32[1,4096]{1,0:T(1,128)S(1)}, u32[]{:S(2)}, u32[]{:S(2)}) collective-permute-start(f32[1,4096]{1,0:T(1,128)S(1)} %get-tuple-element.33), channel_id=1, source_target_pairs={{0,4},{4,8},{8,12},{12,16},{16,20},{20,24},{24,28},{1,5},{5,9},{9,... | collective-permute-start | bytes 49160 | tf_op jit(solution)/shard_map/ppermute | solution.py:22
  90.6 91.4 %collective-permute-start.6 = (f32[1,4096]{1,0:T(1,128)S(1)}, f32[1,4096]{1,0:T(1,128)S(1)}, u32[]{:S(2)}, u32[]{:S(2)}) collective-permute-start(f32[1,4096]{1,0:T(1,128)S(1)} %get-tuple-element.34), channel_id=1, source_target_pairs={{4,0},{8,4},{12,8},{16,12},{20,16},{24,20},{28,24},{5,1},{9,5},{13... | collective-permute-start | bytes 49160 | tf_op jit(solution)/shard_map/ppermute | solution.py:25
  171.2 10.7 %copy-start.10 = (f32[128,4096]{1,0:T(8,128)S(1)}, f32[128,4096]{1,0:T(8,128)}, u32[]{:S(2)}) copy-start(f32[128,4096]{1,0:T(8,128)} %copy-done.9) | copy-start | bytes 6291460
  175.5 7.2 %collective-permute-start.3 = (f32[1,4096]{1,0:T(1,128)S(1)}, f32[1,4096]{1,0:T(1,128)S(1)}, u32[]{:S(2)}, u32[]{:S(2)}) collective-permute-start(f32[1,4096]{1,0:T(1,128)S(1)} %get-tuple-element.35), channel_id=1, source_target_pairs={{0,4},{4,8},{8,12},{12,16},{16,20},{20,24},{24,28},{1,5},{5,9},{9,... | collective-permute-start | bytes 49160 | tf_op jit(solution)/shard_map/ppermute | solution.py:22
  177.4 6.0 %collective-permute-start.4 = (f32[1,4096]{1,0:T(1,128)S(1)}, f32[1,4096]{1,0:T(1,128)S(1)}, u32[]{:S(2)}, u32[]{:S(2)}) collective-permute-start(f32[1,4096]{1,0:T(1,128)S(1)} %get-tuple-element.36), channel_id=1, source_target_pairs={{4,0},{8,4},{12,8},{16,12},{20,16},{24,20},{28,24},{5,1},{9,5},{13... | collective-permute-start | bytes 49160 | tf_op jit(solution)/shard_map/ppermute | solution.py:25
  186.2 8.7 %copy-start.2 = (f32[2,128,4096]{2,1,0:T(8,128)S(1)}, f32[2,128,4096]{2,1,0:T(8,128)}, u32[]{:S(2)}) copy-start(f32[2,128,4096]{2,1,0:T(8,128)} %param.10) | copy-start | bytes 12582916
  186.2 8.7 %copy-start.7 = (f32[2,128,4096]{2,1,0:T(8,128)S(1)}, f32[2,128,4096]{2,1,0:T(8,128)}, u32[]{:S(2)}) copy-start(f32[2,128,4096]{2,1,0:T(8,128)} %convert_element_type.23) | copy-start | bytes 12582916
  188.0 11.7 %collective-permute-start.7 = (f32[1,4096]{1,0:T(1,128)S(1)}, f32[1,4096]{1,0:T(1,128)S(1)}, u32[]{:S(2)}, u32[]{:S(2)}) collective-permute-start(f32[1,4096]{1,0:T(1,128)S(1)} %get-tuple-element.31), channel_id=1, source_target_pairs={{0,4},{4,8},{8,12},{12,16},{16,20},{20,24},{24,28},{1,5},{5,9},{9,... | collective-permute-start | bytes 49160 | tf_op jit(solution)/shard_map/ppermute | solution.py:22
  190.8 9.0 %collective-permute-start.8 = (f32[1,4096]{1,0:T(1,128)S(1)}, f32[1,4096]{1,0:T(1,128)S(1)}, u32[]{:S(2)}, u32[]{:S(2)}) collective-permute-start(f32[1,4096]{1,0:T(1,128)S(1)} %get-tuple-element.32), channel_id=1, source_target_pairs={{4,0},{8,4},{12,8},{16,12},{20,16},{24,20},{28,24},{5,1},{9,5},{13... | collective-permute-start | bytes 49160 | tf_op jit(solution)/shard_map/ppermute | solution.py:25
  202.6 6.2 %copy-start.3 = (f32[2,128,4096]{2,1,0:T(8,128)S(1)}, f32[2,128,4096]{2,1,0:T(8,128)}, u32[]{:S(2)}) copy-start(f32[2,128,4096]{2,1,0:T(8,128)} %get-tuple-element.20) | copy-start | bytes 12582916
  202.6 6.2 %copy-start.15 = (f32[128,4096]{1,0:T(8,128)S(1)}, f32[128,4096]{1,0:T(8,128)}, u32[]{:S(2)}) copy-start(f32[128,4096]{1,0:T(8,128)} %param.16) | copy-start | bytes 6291460
  204.4 5.0 %collective-permute-start.10 = (f32[1,4096]{1,0:T(1,128)S(1)}, f32[1,4096]{1,0:T(1,128)S(1)}, u32[]{:S(2)}, u32[]{:S(2)}) collective-permute-start(f32[1,4096]{1,0:T(1,128)S(1)} %get-tuple-element.30), channel_id=1, source_target_pairs={{4,0},{8,4},{12,8},{16,12},{20,16},{24,20},{28,24},{5,1},{9,5},{13... | collective-permute-start | bytes 49160 | tf_op jit(solution)/shard_map/ppermute | solution.py:25
  206.8 6.0 %collective-permute-start.9 = (f32[1,4096]{1,0:T(1,128)S(1)}, f32[1,4096]{1,0:T(1,128)S(1)}, u32[]{:S(2)}, u32[]{:S(2)}) collective-permute-start(f32[1,4096]{1,0:T(1,128)S(1)} %get-tuple-element.29), channel_id=1, source_target_pairs={{0,4},{4,8},{8,12},{12,16},{16,20},{20,24},{24,28},{1,5},{5,9},{9,... | collective-permute-start | bytes 49160 | tf_op jit(solution)/shard_map/ppermute | solution.py:22
  217.4 11.9 %copy-start.4 = (f32[128,4096]{1,0:T(8,128)}, f32[128,4096]{1,0:T(8,128)S(1)}, u32[]{:S(2)}) copy-start(f32[128,4096]{1,0:T(8,128)S(1)} %slice_add_fusion.2) | copy-start | bytes 6291460
  217.5 11.8 %collective-permute-start.11 = (f32[1,4096]{1,0:T(1,128)S(1)}, f32[1,4096]{1,0:T(1,128)S(1)}, u32[]{:S(2)}, u32[]{:S(2)}) collective-permute-start(f32[1,4096]{1,0:T(1,128)S(1)} %get-tuple-element.27), channel_id=1, source_target_pairs={{0,4},{4,8},{8,12},{12,16},{16,20},{20,24},{24,28},{1,5},{5,9},{9,... | collective-permute-start | bytes 49160 | tf_op jit(solution)/shard_map/ppermute | solution.py:22
  219.4 9.9 %collective-permute-start.12 = (f32[1,4096]{1,0:T(1,128)S(1)}, f32[1,4096]{1,0:T(1,128)S(1)}, u32[]{:S(2)}, u32[]{:S(2)}) collective-permute-start(f32[1,4096]{1,0:T(1,128)S(1)} %get-tuple-element.28), channel_id=1, source_target_pairs={{4,0},{8,4},{12,8},{16,12},{20,16},{24,20},{28,24},{5,1},{9,5},{13... | collective-permute-start | bytes 49160 | tf_op jit(solution)/shard_map/ppermute | solution.py:25
Sparse Core Ops, SparseCore 0:
  85.4 85.7 all-reduce.9
where the time goes:
time: 257 us; the launch traced here: 256 us
  waiting for transfers between devices  125 us (49%)
  other arithmetic  72.3 us (28%)
  starting transfers between devices  36.6 us (14%)
  between operations  14.6 us (6%)
  local copies, waits for them, and re-layouts  8.08 us (3%)
    psum x1, waiting for transfers between devices, body(): summed_flux = lax.psum(bed_change, 'layer')  73.6 us
    ppermute x1, waiting for transfers between devices, passed_along(): return lax.ppermute(block, axis, route)  42.6 us
    ppermute x6, starting transfers between devices, padded(): lax.ppermute(lax.slice_in_dim(block, 0, width, axis=dim), axis, backward)  22.2 us
    ppermute x6, starting transfers between devices, padded(): lax.ppermute(lax.slice_in_dim(block, block.shape[dim] - width, None, axis...  12.8 us
    div x1, other arithmetic, body(): return (settled * (water_depth / new_depth), height)  9.16 us
    reduce_sum x1, other arithmetic, body(): jnp.sum(spread, 0)  8.31 us
    ppermute x6, waiting for transfers between devices, padded(): lax.ppermute(lax.slice_in_dim(block, block.shape[dim] - width, None, axis...  7.76 us
    add x2, other arithmetic, face_divergence(): jnp.maximum(face_speed, 0.0) * left_val  7.51 us
  transfers between devices with their start and end apart: 14, of which 5 were waited for; matrix products, arithmetic and copies ran while one was open for 9% of the time, Pallas kernels for 0%

commit v1 on v0

v1 whole, which is shorter than its diff:
```python
import functools

import jax
import jax.numpy as jnp
from jax import lax
from jax.experimental import pallas as pl
from jax.experimental.pallas import tpu as pltpu
from jax.sharding import PartitionSpec as P

SWEEPS = 4
ADVECT_RATE = 0.1
FLUX_GAIN = 0.15
POROSITY_GAIN = 1.0 / 0.6
RELAX_RATE = 0.2
CRIT_SLOPE = 0.5
DEPTH_FLOOR = 1.0

CH = 16
PAD = 8
SLOTS = 4
LAG = 1
MESH = pl.DeviceIdType.MESH


def down_rows(x, first):
    row = lax.broadcasted_iota(jnp.int32, x.shape, 0)
    return jnp.where(row == 0, first, pltpu.roll(x, 1, 0))


def up_rows(x, last):
    n = x.shape[0]
    row = lax.broadcasted_iota(jnp.int32, x.shape, 0)
    return jnp.where(row == n - 1, last, pltpu.roll(x, n - 1, 0))


def from_left(x):
    col = lax.broadcasted_iota(jnp.int32, x.shape, 1)
    return jnp.where(col == 0, 0.0, pltpu.roll(x, 1, 1))


def from_right(x):
    w = x.shape[1]
    col = lax.broadcasted_iota(jnp.int32, x.shape, 1)
    return jnp.where(col == w - 1, 0.0, pltpu.roll(x, w - 1, 1))


def face(speed_a, speed_b, val_a, val_b):
    f = 0.5 * (speed_a + speed_b)
    return jnp.maximum(f, 0.0) * val_a + jnp.minimum(f, 0.0) * val_b


def move(drop, wet_a, wet_b):
    return RELAX_RATE * (drop - jnp.clip(drop, -CRIT_SLOPE, CRIT_SLOPE)) * wet_a * wet_b


def kernel(
    nb, nl, c_hbm, u_hbm, v_hbm, sett_hbm, surf_hbm, bed_hbm, eros_hbm, wet_hbm,
    out, out_h,
    cs, us, vs, es, ws, ce, ue, we, sett, surf, bed, wetp, ha, hb, dbuf, ubuf, cup,
    edge_out, halo, prv, nxt,
    ring_sem, edge_sem, full_sem, halo_ss, halo_rs, wet_ss, wet_rs, h_ss, h_rs,
    d_ss, d_rs, u_ss, u_rs, c_ss, c_rs,
):
    lh, rows, width = c_hbm.shape
    n = rows // CH
    layers = lh * nl
    l = lax.axis_index("layer")
    b = lax.axis_index("bed")
    has_dn, has_up = l > 0, l < nl - 1
    has_lo, has_hi = b > 0, b < nb - 1
    bottom = (l == 0).astype(jnp.float32)
    neighbours = (
        (has_lo, (b - 1, l)), (has_hi, (b + 1, l)), (has_dn, (b, l - 1)), (has_up, (b, l + 1)),
    )

    def ds(k, size=CH, off=0):
        return pl.ds(pl.multiple_of(k * CH + off, 8), size)

    edges = []
    for side, (start8, start16) in enumerate(((0, 0), (rows - 8, rows - 16))):
        edges.append((
            pltpu.make_async_copy(c_hbm.at[:, pl.ds(start8, 8)], ce.at[side], edge_sem.at[side, 0]),
            pltpu.make_async_copy(u_hbm.at[:, pl.ds(start16, 16)], ue.at[side], edge_sem.at[side, 1]),
            pltpu.make_async_copy(wet_hbm.at[pl.ds(start8, 8)], we.at[side], edge_sem.at[side, 2]),
        ))
    fulls = [
        pltpu.make_async_copy(src, dst, full_sem.at[i])
        for i, (src, dst) in enumerate(((surf_hbm, surf), (bed_hbm, bed), (sett_hbm, sett)))
    ]

    def ring(k):
        s = lax.rem(k, SLOTS)
        return (
            pltpu.make_async_copy(c_hbm.at[:, ds(k)], cs.at[s], ring_sem.at[s, 0]),
            pltpu.make_async_copy(u_hbm.at[:, ds(k)], us.at[s], ring_sem.at[s, 1]),
            pltpu.make_async_copy(v_hbm.at[:, ds(k)], vs.at[s], ring_sem.at[s, 2]),
            pltpu.make_async_copy(eros_hbm.at[ds(k)], es.at[s], ring_sem.at[s, 3]),
            pltpu.make_async_copy(wet_hbm.at[ds(k)], ws.at[s], ring_sem.at[s, 4]),
        )

    for group in edges:
        for copy in group:
            copy.start()
    for copy in fulls:
        copy.start()
    for k in range(min(SLOTS - 1, n)):
        for copy in ring(k):
            copy.start()

    def remote(src, dst, ss, rs, target):
        return pltpu.make_async_remote_copy(
            src_ref=src, dst_ref=dst, send_sem=ss, recv_sem=rs, device_id=target,
            device_id_type=MESH,
        )

    def halo_copy(side):
        return remote(
            edge_out.at[side], halo.at[1 - side], halo_ss.at[side], halo_rs.at[1 - side],
            (b - 1 + 2 * side, l),
        )

    pad_src = (PAD, rows)
    pad_dst = (PAD + rows, 0)

    def wet_copy(side):
        return remote(
            wetp.at[pl.ds(pad_src[side], PAD)], wetp.at[pl.ds(pad_dst[side], PAD)],
            wet_ss.at[side], wet_rs.at[1 - side], (b - 1 + 2 * side, l),
        )

    def height_copy(side):
        return remote(
            ha.at[pl.ds(pad_src[side], PAD)], ha.at[pl.ds(pad_dst[side], PAD)],
            h_ss.at[side], h_rs.at[1 - side], (b - 1 + 2 * side, l),
        )

    def sum_down(k):
        return remote(dbuf.at[ds(k)], dbuf.at[ds(k)], d_ss.at[k], d_rs.at[k], (b, l - 1))

    def sum_up(k):
        return remote(ubuf.at[ds(k)], ubuf.at[ds(k)], u_ss.at[k], u_rs.at[k], (b, l + 1))

    def conc_down(k):
        return remote(c_hbm.at[0, ds(k)], cup.at[ds(k)], c_ss.at[k], c_rs.at[k], (b, l - 1))

    present = (has_lo, has_hi)

    barrier = pltpu.get_barrier_semaphore()
    for there, target in neighbours:
        @pl.when(there)
        def _():
            pl.semaphore_signal(barrier, inc=1, device_id=target, device_id_type=MESH)
    pl.semaphore_wait(barrier, sum(there.astype(jnp.int32) for there, _ in neighbours))

    def start_conc(k):
        @pl.when(has_dn & (k < n))
        def _():
            conc_down(k).start()

    ahead = nl - 1 - l

    start_conc(jnp.int32(0))

    for copy in fulls:
        copy.wait()
    for side in range(2):
        for copy in edges[side]:
            copy.wait()
        row8, row16, row = ((0, 0, 0), (7, 15, rows - 1))[side]
        thick = (surf[row:row + 1, :] - bed[row:row + 1, :]) / layers
        for m in range(lh):
            c = ce[side, m, row8:row8 + 1, :]
            u = ue[side, m].astype(jnp.float32)[row16:row16 + 1, :]
            edge_out[side, m:m + 1, :] = c
            edge_out[side, lh + m:lh + m + 1, :] = u
            edge_out[side, 2 * lh + m:2 * lh + m + 1, :] = u * c * thick
        for row in range(3 * lh, 8):
            edge_out[side, row:row + 1, :] = jnp.zeros((1, width), jnp.float32)
        wetp[pl.ds(pad_src[side], PAD), :] = we[side].astype(jnp.float32)

        @pl.when(present[side])
        def _():
            halo_copy(side).start()
            wet_copy(side).start()

        @pl.when(jnp.logical_not(present[side]))
        def _():
            zeros = jnp.zeros((8, width), jnp.float32)
            halo[side] = zeros
            wetp[pl.ds((0, PAD + rows)[side], PAD), :] = zeros
            ha[pl.ds((0, PAD + rows)[side], PAD), :] = zeros

    def wait_halo(side):
        @pl.when(present[side])
        def _():
            halo_copy(1 - side).wait_recv()

    def flux(k):
        slot = lax.rem(k, SLOTS)
        after = lax.rem(k + 1, SLOTS)

        @pl.when(k + SLOTS - 1 < n)
        def _():
            for copy in ring(k + SLOTS - 1):
                copy.start()

        @pl.when(k == 0)
        def _():
            for copy in ring(k):
                copy.wait()
            wait_halo(0)
            prv[...] = halo[0]

        @pl.when(k < n - 1)
        def _():
            for copy in ring(k + 1):
                copy.wait()
            thick = ((surf[ds(k + 1, 8), :] - bed[ds(k + 1, 8), :]) / layers)[:1]
            for m in range(lh):
                c = cs[after, m, 0:1, :]
                u = us[after, m].astype(jnp.float32)[:1]
                nxt[m:m + 1, :] = c
                nxt[lh + m:lh + m + 1, :] = u
                nxt[2 * lh + m:2 * lh + m + 1, :] = u * c * thick

        @pl.when(k == n - 1)
        def _():
            wait_halo(1)
            nxt[...] = halo[1]

        @pl.when((k > 0) & (k < n - 1))
        def _():
            wetp[ds(k, CH, PAD), :] = ws[slot].astype(jnp.float32)

        @pl.when(k == 0)
        def _():
            wetp[PAD + 8:PAD + CH, :] = ws[slot, 8:, :].astype(jnp.float32)

        @pl.when(k == n - 1)
        def _():
            wetp[PAD + rows - CH:PAD + rows - 8, :] = ws[slot, :8, :].astype(jnp.float32)

        depth = surf[ds(k), :] - bed[ds(k), :]
        thick = depth / layers
        settle = sett[ds(k), :]
        erode = es[slot]
        inverse = layers / depth
        total = None
        col = lax.broadcasted_iota(jnp.int32, (CH, width), 1)
        for m in range(lh):
            c = cs[slot, m]
            u = us[slot, m].astype(jnp.float32)
            v = vs[slot, m].astype(jnp.float32)
            q = u * c * thick
            cn, un, qn = nxt[m:m + 1, :], nxt[lh + m:lh + m + 1, :], nxt[2 * lh + m:2 * lh + m + 1, :]
            cp, up, qp = prv[m:m + 1, :], prv[lh + m:lh + m + 1, :], prv[2 * lh + m:2 * lh + m + 1, :]
            low = face(down_rows(u, up), u, down_rows(c, cp), c)
            high = up_rows(low, face(u[CH - 1:], un, c[CH - 1:], cn))
            left = face(from_left(v), v, from_left(c), c)
            right = jnp.where(
                col == width - 1, jnp.maximum(0.5 * v, 0.0) * c, pltpu.roll(left, width - 1, 1)
            )
            advect = high - low + right - left
            fall = -settle * c
            if m < lh - 1:
                source = settle * cs[slot, m + 1] + fall
            else:
                source = fall
            if m == 0:
                source = source + bottom * erode
            out[m, ds(k), :] = c - ADVECT_RATE * advect + inverse * source
            p = v * c * thick
            spread = 0.5 * (up_rows(q, qn) - down_rows(q, qp) + from_right(p) - from_left(p))
            term = FLUX_GAIN * spread
            if m == 0:
                term = term + bottom * (fall + erode)
            total = term if total is None else total + term
            prv[m:m + 1, :] = c[CH - 1:]
            prv[lh + m:lh + m + 1, :] = u[CH - 1:]
            prv[2 * lh + m:2 * lh + m + 1, :] = q[CH - 1:]
        ha[ds(k, CH, PAD), :] = total

    def tick(t, _):
        @pl.when((t < ahead) & (t > 0))
        def _():
            start_conc(t)

        @pl.when(t < n)
        def _():
            flux(t)

        kd = t - ahead
        ku = t - l - LAG

        @pl.when((kd >= 0) & (kd < n))
        def _():
            @pl.when(has_up)
            def _():
                sum_down(kd).wait_recv()
                dbuf[ds(kd), :] += ha[ds(kd, CH, PAD), :]

            @pl.when(jnp.logical_not(has_up))
            def _():
                dbuf[ds(kd), :] = ha[ds(kd, CH, PAD), :]

            @pl.when(has_dn)
            def _():
                sum_down(kd).start()

            @pl.when(lax.rem(kd, 2) == 1)
            def _():
                start_conc(jnp.maximum(ahead, 1) + lax.div(kd, 2))

        @pl.when(kd == n - 1)
        def _():
            def rest(k, _):
                start_conc(k)
                return 0

            lax.fori_loop(jnp.maximum(ahead, 1) + n // 2, n, rest, 0)

        @pl.when((ku >= 0) & (ku < n))
        def _():
            @pl.when(has_dn)
            def _():
                sum_up(ku).wait_recv()
                ubuf[ds(ku), :] += ha[ds(ku, CH, PAD), :]

            @pl.when(jnp.logical_not(has_dn))
            def _():
                ubuf[ds(ku), :] = ha[ds(ku, CH, PAD), :]

            @pl.when(has_up)
            def _():
                sum_up(ku).start()

        return 0

    lax.fori_loop(0, n + nl - 1 + LAG, tick, 0)

    def first_height(k, _):
        total = dbuf[ds(k), :] + ubuf[ds(k), :] - ha[ds(k, CH, PAD), :]
        ha[ds(k, CH, PAD), :] = bed[ds(k), :] - POROSITY_GAIN * wetp[ds(k, CH, PAD), :] * total
        return 0

    lax.fori_loop(0, n, first_height, 0)
    for side in range(2):
        @pl.when(present[side])
        def _():
            height_copy(side).start()
    for side in range(2):
        @pl.when(present[side])
        def _():
            height_copy(1 - side).wait_recv()
            wet_copy(1 - side).wait_recv()
            height_copy(side).wait_send()

    def slide(src, dst, first, last, shift):
        def block(i, _):
            here = pl.ds(pl.multiple_of(i * 8, 8), 8)
            low = jnp.maximum(i * 8 - 1, 0)
            high = jnp.minimum(i * 8 + 8, rows + 2 * PAD - 1)
            h, w = src[here, :], wetp[here, :]
            hp, wp = src[pl.ds(low, 1), :], wetp[pl.ds(low, 1), :]
            hn, wn = src[pl.ds(high, 1), :], wetp[pl.ds(high, 1), :]
            ml = move(down_rows(h, hp) - h, down_rows(w, wp), w)
            mh = up_rows(ml, move(h[7:] - hn, w[7:], wn))
            yl = move(from_left(h) - h, from_left(w), w)
            yr = pltpu.roll(yl, width - 1, 1)
            dst[pl.ds(pl.multiple_of(i * 8 - shift, 8), 8), :] = h - mh + ml - yr + yl
            return 0

        lax.fori_loop(first, last, block, 0)

    blocks = (rows + 2 * PAD) // 8
    src, dst = ha, hb
    for sweep in range(SWEEPS - 1):
        slide(src, dst, 0, blocks, 0)
        src, dst = dst, src
    slide(src, out_h, 1, blocks - 1, PAD)

    def sent(k, _):
        @pl.when(has_dn)
        def _():
            sum_down(k).wait_send()

        return 0

    lax.fori_loop(0, n, sent, 0)

    def scale(k, _):
        depth = surf[ds(k), :] - bed[ds(k), :]
        new_depth = jnp.maximum(surf[ds(k), :] - out_h[ds(k), :], DEPTH_FLOOR)
        ratio = depth / new_depth
        for m in range(lh):
            out[m, ds(k), :] = out[m, ds(k), :] * ratio
        dbuf[ds(k), :] = layers * sett[ds(k), :] / new_depth
        return 0

    lax.fori_loop(0, n, scale, 0)

    def finish(k, _):
        @pl.when(has_up)
        def _():
            conc_down(k).wait_recv()
            out[lh - 1, ds(k), :] = out[lh - 1, ds(k), :] + dbuf[ds(k), :] * cup[ds(k), :]
            sum_up(k).wait_send()

        @pl.when(has_dn)
        def _():
            conc_down(k).wait_send()

        return 0

    lax.fori_loop(0, n, finish, 0)
    for side in range(2):
        @pl.when(present[side])
        def _():
            halo_copy(side).wait_send()
            wet_copy(side).wait_send()


def body(
    concentration, east_velocity, north_velocity, settling, surface, bed_level, erosion, wet_mask
):
    lh, rows, width = concentration.shape
    nb, nl = lax.axis_size("bed"), lax.axis_size("layer")
    n = rows // CH
    f32, bf16 = jnp.float32, jnp.bfloat16
    tall = rows + 2 * PAD
    vmem = pltpu.VMEM
    dma = pltpu.SemaphoreType.DMA
    cells = lh * rows * width
    return pl.pallas_call(
        functools.partial(kernel, nb, nl),
        out_shape=(
            jax.ShapeDtypeStruct((lh, rows, width), f32),
            jax.ShapeDtypeStruct((rows, width), f32),
        ),
        in_specs=[pl.BlockSpec(memory_space=pl.ANY)] * 8,
        out_specs=[pl.BlockSpec(memory_space=pltpu.VMEM)] * 2,
        scratch_shapes=[
            vmem((SLOTS, lh, CH, width), f32),
            vmem((SLOTS, lh, CH, width), bf16),
            vmem((SLOTS, lh, CH, width), bf16),
            vmem((SLOTS, CH, width), f32),
            vmem((SLOTS, CH, width), jnp.int32),
            vmem((2, lh, 8, width), f32),
            vmem((2, lh, 16, width), bf16),
            vmem((2, 8, width), jnp.int32),
            vmem((rows, width), f32),
            vmem((rows, width), f32),
            vmem((rows, width), f32),
            vmem((tall, width), f32),
            vmem((tall, width), f32),
            vmem((tall, width), f32),
            vmem((rows, width), f32),
            vmem((rows, width), f32),
            vmem((rows, width), f32),
            vmem((2, 8, width), f32),
            vmem((2, 8, width), f32),
            vmem((8, width), f32),
            vmem((8, width), f32),
            dma((SLOTS, 5)),
            dma((2, 3)),
            dma((3,)),
            dma((2,)), dma((2,)),
            dma((2,)), dma((2,)),
            dma((2,)), dma((2,)),
            dma((n,)), dma((n,)),
            dma((n,)), dma((n,)),
            dma((n,)), dma((n,)),
        ],
        compiler_params=pltpu.CompilerParams(
            collective_id=0, has_side_effects=True, vmem_limit_bytes=63 << 20
        ),
        cost_estimate=pl.CostEstimate(
            flops=100 * cells, bytes_accessed=24 * cells, transcendentals=0
        ),
    )(
        concentration, east_velocity, north_velocity, settling, surface, bed_level, erosion,
        wet_mask,
    )


def solution(mesh):
    layered = P("layer", "bed", None)
    flat = P("bed", None)
    return jax.shard_map(
        body, mesh=mesh, in_specs=(layered,) * 3 + (flat,) * 5, out_specs=(layered, flat),
        check_vma=False,
    )
```

time: 257 us -> 126 us (0.49)
  the two profiles are of different devices: /device:TPU:4 before, /device:TPU:27 now
where the time goes in v1:
time: 126 us
  Pallas kernels  119 us (94%)
  local copies, waits for them, and re-layouts  6.13 us (5%)
    pallas_call x1, Pallas kernels, body(): pl.pallas_call(functools.partial(kernel, nb, nl), out_shape=(jax.ShapeDty...  119 us
    unnamed x4, local copies, waits for them, and re-layouts  6.13 us

profile of v1, /device:TPU:27, one launch (start us, length us, event | category | flops | bytes accessed | tf_op | source)
XLA Modules:
  0.0 125.8 jit_solution(13436791225661102381)
XLA Ops:
  0.6 119.1 %shard_map.95 = (f32[2,128,4096]{2,1,0:T(8,128)}, f32[128,4096]{1,0:T(8,128)}) custom-call(f32[2,128,4096]{2,1,0:T(8,128)} %c_hbm.1, bf16[2,128,4096]{2,1,0:T(8,128)(2,1)} %u_hbm.1, bf16[2,128,4096]{2,1,0:T(8,128)(2,1)} %v_hbm.1, f32[128,4096]{1,0:T(8,128)} %sett_hbm.1, f32[128,4096]{1,0:T(8,128)} %surf_hbm.1, f32[128,4096]{1,0:T(8,128)} %bed_hbm.1, ...), custom_call_target="tpu_custom_call" | custom-call | flops 104857600 | bytes 25165824 | tf_op jit(solution)/shard_map/pallas_call | solution.py:434
  119.7 0.0 copy-start
  119.7 4.8 %copy.12 = f32[2,128,4096]{2,1,0:T(8,128)} copy(f32[2,128,4096]{2,1,0:T(8,128)} %get-tuple-element.4) | data formatting | bytes 8388608
  124.5 0.0 copy-done
  124.5 1.3 %copy.13 = f32[128,4096]{1,0:T(8,128)} copy(f32[128,4096]{1,0:T(8,128)S(1)} %copy-done) | data formatting | bytes 4194304
Async XLA Ops:
  119.7 4.8 %copy-start = (f32[128,4096]{1,0:T(8,128)S(1)}, f32[128,4096]{1,0:T(8,128)}, u32[]{:S(2)}) copy-start(f32[128,4096]{1,0:T(8,128)} %get-tuple-element.5) | copy-start | bytes 6291460

commit v2 on v1

--- a/solution.py
+++ b/solution.py
@@ -18,7 +18,11 @@
 CH = 16
 PAD = 8
 SLOTS = 4
-LAG = 1
+CD = 8
+LEAD, LEAD_HOP = 1, 1
+EVERY = 99
+HOP = 2
+LAG = 0
 MESH = pl.DeviceIdType.MESH
 
 
@@ -49,20 +53,22 @@
     return jnp.maximum(f, 0.0) * val_a + jnp.minimum(f, 0.0) * val_b
 
 
-def move(drop, wet_a, wet_b):
-    return RELAX_RATE * (drop - jnp.clip(drop, -CRIT_SLOPE, CRIT_SLOPE)) * wet_a * wet_b
+def move(drop, weight):
+    return (drop - jnp.clip(drop, -CRIT_SLOPE, CRIT_SLOPE)) * weight
 
 
 def kernel(
     nb, nl, c_hbm, u_hbm, v_hbm, sett_hbm, surf_hbm, bed_hbm, eros_hbm, wet_hbm,
-    out, out_h,
-    cs, us, vs, es, ws, ce, ue, we, sett, surf, bed, wetp, ha, hb, dbuf, ubuf, cup,
+    out_hbm, out_h_hbm,
+    out, out_h, wx, wy, cs, us, vs, es, ws, ce, ue, we, sett, surf, bed, wetp, ha, hb, dbuf, ubuf, cup,
     edge_out, halo, prv, nxt,
     ring_sem, edge_sem, full_sem, halo_ss, halo_rs, wet_ss, wet_rs, h_ss, h_rs,
-    d_ss, d_rs, u_ss, u_rs, c_ss, c_rs,
+    d_ss, d_rs, u_ss, u_rs, c_ss, c_rs, out_sem, early_sem,
 ):
     lh, rows, width = c_hbm.shape
     n = rows // CH
+    nd = rows // CD
+    per = CH // CD
     layers = lh * nl
     l = lax.axis_index("layer")
     b = lax.axis_index("bed")
@@ -75,6 +81,9 @@
 
     def ds(k, size=CH, off=0):
         return pl.ds(pl.multiple_of(k * CH + off, 8), size)
+
+    def dd(k, off=0):
+        return pl.ds(pl.multiple_of(k * CD + off, 8), CD)
 
     edges = []
     for side, (start8, start16) in enumerate(((0, 0), (rows - 8, rows - 16))):
@@ -135,10 +144,10 @@
         )
 
     def sum_down(k):
-        return remote(dbuf.at[ds(k)], dbuf.at[ds(k)], d_ss.at[k], d_rs.at[k], (b, l - 1))
+        return remote(dbuf.at[dd(k)], dbuf.at[dd(k)], d_ss.at[k], d_rs.at[k], (b, l - 1))
 
     def sum_up(k):
-        return remote(ubuf.at[ds(k)], ubuf.at[ds(k)], u_ss.at[k], u_rs.at[k], (b, l + 1))
+        return remote(ubuf.at[dd(k)], ubuf.at[dd(k)], u_ss.at[k], u_rs.at[k], (b, l + 1))
 
     def conc_down(k):
         return remote(c_hbm.at[0, ds(k)], cup.at[ds(k)], c_ss.at[k], c_rs.at[k], (b, l - 1))
@@ -158,8 +167,16 @@
             conc_down(k).start()
 
     ahead = nl - 1 - l
-
-    start_conc(jnp.int32(0))
+    lead = jnp.minimum(LEAD + LEAD_HOP * ahead, n)
+
+    def send_conc(first, last):
+        def one(k, _):
+            start_conc(k)
+            return 0
+
+        lax.fori_loop(first, last, one, 0)
+
+    send_conc(0, lead)
 
     for copy in fulls:
         copy.wait()
@@ -280,63 +297,72 @@
             prv[2 * lh + m:2 * lh + m + 1, :] = q[CH - 1:]
         ha[ds(k, CH, PAD), :] = total
 
+    def weigh(i):
+        here = pl.ds(pl.multiple_of(i * 8, 8), 8)
+        w = wetp[here, :]
+        wx[here, :] = RELAX_RATE * w * down_rows(w, wetp[pl.ds(jnp.maximum(i * 8 - 1, 0), 1), :])
+        wy[here, :] = RELAX_RATE * w * from_left(w)
+
     def tick(t, _):
-        @pl.when((t < ahead) & (t > 0))
-        def _():
-            start_conc(t)
-
-        @pl.when(t < n)
-        def _():
-            flux(t)
-
-        kd = t - ahead
-        ku = t - l - LAG
-
-        @pl.when((kd >= 0) & (kd < n))
+        @pl.when((t < nd) & (lax.rem(t, per) == 0))
+        def _():
+            flux(lax.div(t, per))
+
+        kd = t - HOP * ahead
+        ku = t - HOP * l - LAG
+
+        @pl.when((kd >= 0) & (kd < nd))
         def _():
             @pl.when(has_up)
             def _():
                 sum_down(kd).wait_recv()
-                dbuf[ds(kd), :] += ha[ds(kd, CH, PAD), :]
+                dbuf[dd(kd), :] += ha[dd(kd, PAD), :]
 
             @pl.when(jnp.logical_not(has_up))
             def _():
-                dbuf[ds(kd), :] = ha[ds(kd, CH, PAD), :]
+                dbuf[dd(kd), :] = ha[dd(kd, PAD), :]
 
             @pl.when(has_dn)
             def _():
                 sum_down(kd).start()
 
-            @pl.when(lax.rem(kd, 2) == 1)
-            def _():
-                start_conc(jnp.maximum(ahead, 1) + lax.div(kd, 2))
-
-        @pl.when(kd == n - 1)
-        def _():
-            def rest(k, _):
-                start_conc(k)
-                return 0
-
-            lax.fori_loop(jnp.maximum(ahead, 1) + n // 2, n, rest, 0)
-
-        @pl.when((ku >= 0) & (ku < n))
+            @pl.when(lax.rem(kd, EVERY) == EVERY - 1)
+            def _():
+                start_conc(lead + lax.div(kd, EVERY))
+
+        @pl.when(kd == nd - 1)
+        def _():
+            send_conc(lead + nd // EVERY, n)
+
+        @pl.when((ku >= 0) & (ku < nd))
         def _():
             @pl.when(has_dn)
             def _():
                 sum_up(ku).wait_recv()
-                ubuf[ds(ku), :] += ha[ds(ku, CH, PAD), :]
+                ubuf[dd(ku), :] += ha[dd(ku, PAD), :]
 
             @pl.when(jnp.logical_not(has_dn))
             def _():
-                ubuf[ds(ku), :] = ha[ds(ku, CH, PAD), :]
+                ubuf[dd(ku), :] = ha[dd(ku, PAD), :]
 
             @pl.when(has_up)
             def _():
                 sum_up(ku).start()
 
+        @pl.when((t >= 2) & (t <= rows // 8))
+        def _():
+            weigh(t)
+
         return 0
 
-    lax.fori_loop(0, n + nl - 1 + LAG, tick, 0)
+    lax.fori_loop(0, nd + HOP * (nl - 1) + LAG, tick, 0)
+
+    for side in range(2):
+        @pl.when(present[side])
+        def _():
+            wet_copy(1 - side).wait_recv()
+    for i in (0, 1, rows // 8 + 1):
+        weigh(jnp.int32(i))
 
     def first_height(k, _):
         total = dbuf[ds(k), :] + ubuf[ds(k), :] - ha[ds(k, CH, PAD), :]
@@ -352,7 +378,6 @@
         @pl.when(present[side])
         def _():
             height_copy(1 - side).wait_recv()
-            wet_copy(1 - side).wait_recv()
             height_copy(side).wait_send()
 
     def slide(src, dst, first, last, shift):
@@ -360,12 +385,11 @@
             here = pl.ds(pl.multiple_of(i * 8, 8), 8)
             low = jnp.maximum(i * 8 - 1, 0)
             high = jnp.minimum(i * 8 + 8, rows + 2 * PAD - 1)
-            h, w = src[here, :], wetp[here, :]
-            hp, wp = src[pl.ds(low, 1), :], wetp[pl.ds(low, 1), :]
-            hn, wn = src[pl.ds(high, 1), :], wetp[pl.ds(high, 1), :]
-            ml = move(down_rows(h, hp) - h, down_rows(w, wp), w)
-            mh = up_rows(ml, move(h[7:] - hn, w[7:], wn))
-            yl = move(from_left(h) - h, from_left(w), w)
+            h, g = src[here, :], wx[here, :]
+            hp, hn = src[pl.ds(low, 1), :], src[pl.ds(high, 1), :]
+            ml = move(down_rows(h, hp) - h, g)
+            mh = up_rows(ml, move(h[7:] - hn, wx[pl.ds(high, 1), :]))
+            yl = move(pltpu.roll(h, 1, 1) - h, wy[here, :])
             yr = pltpu.roll(yl, width - 1, 1)
             dst[pl.ds(pl.multiple_of(i * 8 - shift, 8), 8), :] = h - mh + ml - yr + yl
             return 0
@@ -379,14 +403,21 @@
         src, dst = dst, src
     slide(src, out_h, 1, blocks - 1, PAD)
 
+    early = [pltpu.make_async_copy(out_h, out_h_hbm, early_sem.at[0])]
+    early[0].start()
+
     def sent(k, _):
         @pl.when(has_dn)
         def _():
             sum_down(k).wait_send()
 
+        @pl.when(has_up)
+        def _():
+            sum_up(k).wait_send()
+
         return 0
 
-    lax.fori_loop(0, n, sent, 0)
+    lax.fori_loop(0, nd, sent, 0)
 
     def scale(k, _):
         depth = surf[ds(k), :] - bed[ds(k), :]
@@ -399,12 +430,24 @@
 
     lax.fori_loop(0, n, scale, 0)
 
+    early += [
+        pltpu.make_async_copy(out.at[m], out_hbm.at[m], early_sem.at[1 + m]) for m in range(lh - 1)
+    ]
+    for copy in early[1:]:
+        copy.start()
+
+    def last_copy(k):
+        return pltpu.make_async_copy(
+            out.at[lh - 1, ds(k)], out_hbm.at[lh - 1, ds(k)], out_sem.at[k]
+        )
+
     def finish(k, _):
         @pl.when(has_up)
         def _():
             conc_down(k).wait_recv()
             out[lh - 1, ds(k), :] = out[lh - 1, ds(k), :] + dbuf[ds(k), :] * cup[ds(k), :]
-            sum_up(k).wait_send()
+
+        last_copy(k).start()
 
         @pl.when(has_dn)
         def _():
@@ -413,11 +456,42 @@
         return 0
 
     lax.fori_loop(0, n, finish, 0)
+    for copy in early:
+        copy.wait()
+
+    def written(k, _):
+        last_copy(k).wait()
+        return 0
+
+    lax.fori_loop(0, n, written, 0)
     for side in range(2):
         @pl.when(present[side])
         def _():
             halo_copy(side).wait_send()
             wet_copy(side).wait_send()
+
+
+def place(conc, height, out, out_h, conc_held, height_held, in_sem, out_sem):
+    lh, rows, _ = conc.shape
+    moves = []
+    for part in range(lh + 1):
+        src, held, dst = (
+            (conc.at[part], conc_held.at[part], out.at[part])
+            if part < lh else (height, height_held, out_h)
+        )
+        for k in range(rows // CH):
+            here = pl.ds(k * CH, CH)
+            moves.append((
+                pltpu.make_async_copy(src.at[here], held.at[here], in_sem.at[part, k]),
+                pltpu.make_async_copy(held.at[here], dst.at[here], out_sem.at[part, k]),
+            ))
+    for fetch, _ in moves:
+        fetch.start()
+    for fetch, store in moves:
+        fetch.wait()
+        store.start()
+    for _, store in moves:
+        store.wait()
 
 
 def body(
@@ -425,21 +499,25 @@
 ):
     lh, rows, width = concentration.shape
     nb, nl = lax.axis_size("bed"), lax.axis_size("layer")
-    n = rows // CH
+    n, nd = rows // CH, rows // CD
     f32, bf16 = jnp.float32, jnp.bfloat16
     tall = rows + 2 * PAD
     vmem = pltpu.VMEM
     dma = pltpu.SemaphoreType.DMA
     cells = lh * rows * width
-    return pl.pallas_call(
+    results = pl.pallas_call(
         functools.partial(kernel, nb, nl),
         out_shape=(
             jax.ShapeDtypeStruct((lh, rows, width), f32),
             jax.ShapeDtypeStruct((rows, width), f32),
         ),
         in_specs=[pl.BlockSpec(memory_space=pl.ANY)] * 8,
-        out_specs=[pl.BlockSpec(memory_space=pltpu.VMEM)] * 2,
+        out_specs=[pl.BlockSpec(memory_space=pl.ANY)] * 2,
         scratch_shapes=[
+            vmem((lh, rows, width), f32),
+            vmem((rows, width), f32),
+            vmem((tall, width), f32),
+            vmem((tall, width), f32),
             vmem((SLOTS, lh, CH, width), f32),
             vmem((SLOTS, lh, CH, width), bf16),
             vmem((SLOTS, lh, CH, width), bf16),
@@ -467,9 +545,10 @@
             dma((2,)), dma((2,)),
             dma((2,)), dma((2,)),
             dma((2,)), dma((2,)),
+            dma((nd,)), dma((nd,)),
+            dma((nd,)), dma((nd,)),
             dma((n,)), dma((n,)),
-            dma((n,)), dma((n,)),
-            dma((n,)), dma((n,)),
+            dma((n,)), dma((lh,)),
         ],
         compiler_params=pltpu.CompilerParams(
             collective_id=0, has_side_effects=True, vmem_limit_bytes=63 << 20
@@ -481,6 +560,22 @@
         concentration, east_velocity, north_velocity, settling, surface, bed_level, erosion,
         wet_mask,
     )
+    return pl.pallas_call(
+        place,
+        out_shape=tuple(jax.ShapeDtypeStruct(r.shape, r.dtype) for r in results),
+        in_specs=[pl.BlockSpec(memory_space=pl.ANY)] * 2,
+        out_specs=[pl.BlockSpec(memory_space=pl.ANY)] * 2,
+        scratch_shapes=[
+            vmem((lh, rows, width), f32),
+            vmem((rows, width), f32),
+            dma((lh + 1, n)),
+            dma((lh + 1, n)),
+        ],
+        compiler_params=pltpu.CompilerParams(vmem_limit_bytes=63 << 20),
+        cost_estimate=pl.CostEstimate(
+            flops=0, bytes_accessed=8 * (cells + rows * width), transcendentals=0
+        ),
+    )(*results)
 
 
 def solution(mesh):

time: 126 us -> 104 us (0.83)
  the two profiles are of different devices: /device:TPU:27 before, /device:TPU:4 now
where the time goes in v2:
time: 104 us; the launch traced here: 102 us
  Pallas kernels  102 us (98%)
    pallas_call x1, Pallas kernels, body(): pl.pallas_call(functools.partial(kernel, nb, nl), out_shape=(jax.ShapeDty...  96.1 us
    pallas_call x1, Pallas kernels, body(): pl.pallas_call(place, out_shape=tuple((jax.ShapeDtypeStruct(r.shape, r.dt...  5.57 us

profile of v2, /device:TPU:4, one launch (start us, length us, event | category | flops | bytes accessed | tf_op | source)
XLA Modules:
  0.0 102.3 jit_solution(568551555413250850)
XLA Ops:
  0.6 96.1 %shard_map.95 = (f32[2,128,4096]{2,1,0:T(8,128)}, f32[128,4096]{1,0:T(8,128)}) custom-call(f32[2,128,4096]{2,1,0:T(8,128)} %c_hbm.1, bf16[2,128,4096]{2,1,0:T(8,128)(2,1)} %u_hbm.1, bf16[2,128,4096]{2,1,0:T(8,128)(2,1)} %v_hbm.1, f32[128,4096]{1,0:T(8,128)} %sett_hbm.1, f32[128,4096]{1,0:T(8,128)} %surf_hbm.1, f32[128,4096]{1,0:T(8,128)} %bed_hbm.1, ...), custom_call_target="tpu_custom_call" | custom-call | flops 104857600 | bytes 25165824 | tf_op jit(solution)/shard_map/pallas_call | solution.py:508
  96.7 5.6 %shard_map.96 = (f32[2,128,4096]{2,1,0:T(8,128)}, f32[128,4096]{1,0:T(8,128)}) custom-call(f32[2,128,4096]{2,1,0:T(8,128)} %get-tuple-element.4.conc, f32[128,4096]{1,0:T(8,128)} %get-tuple-element.5.height), custom_call_target="tpu_custom_call" | custom-call | bytes 12582912 | tf_op jit(solution)/shard_map/pallas_call | solution.py:563

commit v3 on v2

--- a/solution.py
+++ b/solution.py
@@ -59,11 +59,10 @@
 
 def kernel(
     nb, nl, c_hbm, u_hbm, v_hbm, sett_hbm, surf_hbm, bed_hbm, eros_hbm, wet_hbm,
-    out_hbm, out_h_hbm,
     out, out_h, wx, wy, cs, us, vs, es, ws, ce, ue, we, sett, surf, bed, wetp, ha, hb, dbuf, ubuf, cup,
     edge_out, halo, prv, nxt,
     ring_sem, edge_sem, full_sem, halo_ss, halo_rs, wet_ss, wet_rs, h_ss, h_rs,
-    d_ss, d_rs, u_ss, u_rs, c_ss, c_rs, out_sem, early_sem,
+    d_ss, d_rs, u_ss, u_rs, c_ss, c_rs,
 ):
     lh, rows, width = c_hbm.shape
     n = rows // CH
@@ -403,9 +402,6 @@
         src, dst = dst, src
     slide(src, out_h, 1, blocks - 1, PAD)
 
-    early = [pltpu.make_async_copy(out_h, out_h_hbm, early_sem.at[0])]
-    early[0].start()
-
     def sent(k, _):
         @pl.when(has_dn)
         def _():
@@ -430,25 +426,12 @@
 
     lax.fori_loop(0, n, scale, 0)
 
-    early += [
-        pltpu.make_async_copy(out.at[m], out_hbm.at[m], early_sem.at[1 + m]) for m in range(lh - 1)
-    ]
-    for copy in early[1:]:
-        copy.start()
-
-    def last_copy(k):
-        return pltpu.make_async_copy(
-            out.at[lh - 1, ds(k)], out_hbm.at[lh - 1, ds(k)], out_sem.at[k]
-        )
-
     def finish(k, _):
         @pl.when(has_up)
         def _():
             conc_down(k).wait_recv()
             out[lh - 1, ds(k), :] = out[lh - 1, ds(k), :] + dbuf[ds(k), :] * cup[ds(k), :]
 
-        last_copy(k).start()
-
         @pl.when(has_dn)
         def _():
             conc_down(k).wait_send()
@@ -456,14 +439,6 @@
         return 0
 
     lax.fori_loop(0, n, finish, 0)
-    for copy in early:
-        copy.wait()
-
-    def written(k, _):
-        last_copy(k).wait()
-        return 0
-
-    lax.fori_loop(0, n, written, 0)
     for side in range(2):
         @pl.when(present[side])
         def _():
@@ -471,27 +446,18 @@
             wet_copy(side).wait_send()
 
 
-def place(conc, height, out, out_h, conc_held, height_held, in_sem, out_sem):
+def place(conc, height, out, out_h, sem):
     lh, rows, _ = conc.shape
     moves = []
     for part in range(lh + 1):
-        src, held, dst = (
-            (conc.at[part], conc_held.at[part], out.at[part])
-            if part < lh else (height, height_held, out_h)
-        )
-        for k in range(rows // CH):
-            here = pl.ds(k * CH, CH)
-            moves.append((
-                pltpu.make_async_copy(src.at[here], held.at[here], in_sem.at[part, k]),
-                pltpu.make_async_copy(held.at[here], dst.at[here], out_sem.at[part, k]),
-            ))
-    for fetch, _ in moves:
-        fetch.start()
-    for fetch, store in moves:
-        fetch.wait()
-        store.start()
-    for _, store in moves:
-        store.wait()
+        src, dst = (conc.at[part], out.at[part]) if part < lh else (height, out_h)
+        for k in range(rows // 32):
+            here = pl.ds(k * 32, 32)
+            moves.append(pltpu.make_async_copy(src.at[here], dst.at[here], sem.at[part, k]))
+    for move_out in moves:
+        move_out.start()
+    for move_out in moves:
+        move_out.wait()
 
 
 def body(
@@ -507,15 +473,10 @@
     cells = lh * rows * width
     results = pl.pallas_call(
         functools.partial(kernel, nb, nl),
-        out_shape=(
-            jax.ShapeDtypeStruct((lh, rows, width), f32),
-            jax.ShapeDtypeStruct((rows, width), f32),
-        ),
-        in_specs=[pl.BlockSpec(memory_space=pl.ANY)] * 8,
-        out_specs=[pl.BlockSpec(memory_space=pl.ANY)] * 2,
+        out_shape=(vmem((lh, rows, width), f32), vmem((rows, width), f32)),
+        in_specs=[pl.BlockSpec(memory_space=pltpu.HBM)] * 8,
+        out_specs=[pl.BlockSpec(memory_space=pltpu.VMEM)] * 2,
         scratch_shapes=[
-            vmem((lh, rows, width), f32),
-            vmem((rows, width), f32),
             vmem((tall, width), f32),
             vmem((tall, width), f32),
             vmem((SLOTS, lh, CH, width), f32),
@@ -548,10 +509,9 @@
             dma((nd,)), dma((nd,)),
             dma((nd,)), dma((nd,)),
             dma((n,)), dma((n,)),
-            dma((n,)), dma((lh,)),
         ],
         compiler_params=pltpu.CompilerParams(
-            collective_id=0, has_side_effects=True, vmem_limit_bytes=63 << 20
+            collective_id=0, has_side_effects=True, vmem_limit_bytes=50 << 20
         ),
         cost_estimate=pl.CostEstimate(
             flops=100 * cells, bytes_accessed=24 * cells, transcendentals=0
@@ -562,16 +522,14 @@
     )
     return pl.pallas_call(
         place,
-        out_shape=tuple(jax.ShapeDtypeStruct(r.shape, r.dtype) for r in results),
-        in_specs=[pl.BlockSpec(memory_space=pl.ANY)] * 2,
-        out_specs=[pl.BlockSpec(memory_space=pl.ANY)] * 2,
-        scratch_shapes=[
-            vmem((lh, rows, width), f32),
-            vmem((rows, width), f32),
-            dma((lh + 1, n)),
-            dma((lh + 1, n)),
-        ],
-        compiler_params=pltpu.CompilerParams(vmem_limit_bytes=63 << 20),
+        out_shape=(
+            jax.ShapeDtypeStruct((lh, rows, width), f32),
+            jax.ShapeDtypeStruct((rows, width), f32),
+        ),
+        in_specs=[pl.BlockSpec(memory_space=pltpu.VMEM)] * 2,
+        out_specs=[pl.BlockSpec(memory_space=pltpu.HBM)] * 2,
+        scratch_shapes=[dma((lh + 1, rows // 32))],
+        compiler_params=pltpu.CompilerParams(vmem_limit_bytes=16 << 20),
         cost_estimate=pl.CostEstimate(
             flops=0, bytes_accessed=8 * (cells + rows * width), transcendentals=0
         ),

time: 104 us -> 100 us (0.962)
  Pallas kernels: 102 us -> 98.1 us
    pallas_call x2, Pallas kernels: 102 us -> 98.1 us  [the longest x1 95.3 us: body(): pl.pallas_call(functools.partial(kernel, nb, nl), out_shape=(vmem((lh, ro...]
where the time goes in v3:
time: 100 us; the launch traced here: 98.7 us
  Pallas kernels  98.1 us (98%)
    pallas_call x1, Pallas kernels, body(): pl.pallas_call(functools.partial(kernel, nb, nl), out_shape=(vmem((lh, ro...  95.3 us
    pallas_call x1, Pallas kernels, body(): pl.pallas_call(place, out_shape=(jax.ShapeDtypeStruct((lh, rows, width),...  2.75 us

profile of v3, /device:TPU:4, one launch (start us, length us, event | category | flops | bytes accessed | tf_op | source)
XLA Modules:
  0.0 98.7 jit_solution(14681966733906121833)
XLA Ops:
  0.6 95.3 %shard_map.95 = (f32[2,128,4096]{2,1,0:T(8,128)S(1)}, f32[128,4096]{1,0:T(8,128)S(1)}) custom-call(f32[2,128,4096]{2,1,0:T(8,128)} %c_hbm.1, bf16[2,128,4096]{2,1,0:T(8,128)(2,1)} %u_hbm.1, bf16[2,128,4096]{2,1,0:T(8,128)(2,1)} %v_hbm.1, f32[128,4096]{1,0:T(8,128)} %sett_hbm.1, f32[128,4096]{1,0:T(8,128)} %surf_hbm.1, f32[128,4096]{1,0:T(8,128)} %bed_hbm.1, ...), custom_call_target="tpu_custom_call" | custom-call | flops 104857600 | bytes 25165824 | tf_op jit(solution)/shard_map/pallas_call | solution.py:474
  96.0 2.8 %shard_map.96 = (f32[2,128,4096]{2,1,0:T(8,128)}, f32[128,4096]{1,0:T(8,128)}) custom-call(f32[2,128,4096]{2,1,0:T(8,128)S(1)} %get-tuple-element.4.conc, f32[128,4096]{1,0:T(8,128)S(1)} %get-tuple-element.5.height), custom_call_target="tpu_custom_call" | custom-call | bytes 12582912 | tf_op jit(solution)/shard_map/pallas_call | solution.py:523
